TPU v7x, 32 devices: a whole 2x2x4 slice. The times are simulated.
32 devices in a mesh: col: 8 (over z, x), sec: 4 (over y, core).
Axes of the slice: x: 2, y: 2, z: 4, core: 2. Of those that a mesh axis runs over, the one named last changes fastest.
Arguments:
- left_start: bfloat16 [2048, 6, 1024], P('sec'), may hold values from -6 to 6
- coupling: bfloat16 [8, 2048, 2304], P('col', 'sec'), may hold values from -0.125 to 0.125
- tensor: float32 [8, 6, 6, 6, 6], P('col'), may hold values from -1 to 1
- sketch: float32 [8, 6, 1024], P('col'), may hold values from -3 to 3
- block_parity: int32 [16], replicated, may hold values from 0 to 1
- leg_parity: int32 [8, 6], replicated, may hold values from 0 to 1, as said below
Outputs:
- states: bfloat16 [8, 2048, 6, 1024], P('col', 'sec')
- grams: float32 [8, 1024, 1024], P('col', 'sec')
Inputs may be any that keep to these rules, and one draw needn't show every extreme that they name: `leg_parity`: in each column exactly half of the 6 leg states are odd.
All inputs are finite; a program needn't handle non-finite values.
Results may differ from a plain program's by a relative error of at most 0.019.
Values may be sent and summed in bfloat16 or wider, within the bound.
No kernel may reach another device: no remote copies, remote signals or barrier semaphores. Data moves between devices by JAX's collectives and lax.ppermute only.
A program may use at most 192 MiB of HBM per device.

v0:
```python
import jax
import jax.numpy as jnp
from jax import lax
from jax.sharding import PartitionSpec as P

CHI = 2048
D = 6
PAN = 128


def padded_2(block, sides, width):
    for axis, dim in sides:
        count = lax.axis_size(axis)
        forward = [(i, i + 1) for i in range(count - 1)]
        backward = [(target, source) for source, target in forward]
        low = lax.ppermute(
            lax.slice_in_dim(block, block.shape[dim] - width, None, axis=dim), axis, forward
        )
        high = lax.ppermute(lax.slice_in_dim(block, 0, width, axis=dim), axis, backward)
        block = jnp.concatenate([low, block, high], axis=dim)
    return block


def shifted(block, axis, distance):
    devices = range(lax.axis_size(axis))
    route = [(i - distance, i) for i in devices if i - distance in devices]
    return lax.ppermute(block, axis, route)


def panel_signs(block_parity, leg_row, first_panel, panel_total):
    padded = jnp.pad(block_parity, (1, 1))
    window = lax.dynamic_slice_in_dim(padded, first_panel, panel_total, 0)
    odd_pairs = window.astype(jnp.float32)[:, None] * leg_row.astype(jnp.float32)[None, :]
    return 1.0 - 2.0 * odd_pairs


def advance(extended, mix_block, band_rows, sign_table):
    panel_total = sign_table.shape[0]
    panel_count = panel_total - 2
    leg_count = mix_block.shape[0]
    width = mix_block.shape[3]
    weighted = jnp.einsum(
        "adk,duek->auek", extended.astype(jnp.float32), mix_block, precision=lax.Precision.HIGHEST
    )
    weighted = weighted.reshape(panel_total, PAN, leg_count, leg_count * width)
    weighted = weighted * sign_table[:, None, :, None]
    weighted = weighted.astype(jnp.bfloat16).reshape(
        panel_total, PAN * leg_count, leg_count * width
    )
    summed = jnp.zeros((panel_count, PAN, leg_count * width), jnp.float32)
    for neighbour in range(3):
        summed = summed + jnp.einsum(
            "pbx,pxm->pbm",
            band_rows[:, :, neighbour],
            weighted[neighbour : neighbour + panel_count],
            preferred_element_type=jnp.float32,
        )
    return summed.astype(jnp.bfloat16).reshape(panel_count * PAN, leg_count, width)


def on_device(left_start, coupling, tensor, sketch, block_parity, leg_parity):
    row_count, leg_count, rank_total = left_start.shape
    panel_count = row_count // PAN
    col_count = lax.axis_size("col")
    sec_count = lax.axis_size("sec")
    col_index = lax.axis_index("col")
    first_panel = lax.axis_index("sec") * panel_count
    own_legs = lax.dynamic_index_in_dim(leg_parity, col_index, 0, keepdims=False)
    sign_table = panel_signs(block_parity, own_legs, first_panel, panel_count + 2)
    block_cols = 128
    block_count = rank_total // block_cols
    step_count = block_count + col_count - 1
    mixing = jnp.einsum("duez,zk->duek", tensor[0], sketch[0], precision=lax.Precision.HIGHEST)
    band_rows = coupling[0].reshape(panel_count, PAN, 3, PAN * leg_count)

    def turn(step_now, carry):
        received, sketch_out = carry
        block_now = step_now - col_index
        active = (block_now >= 0) & (block_now < block_count)
        offset = jnp.clip(block_now, 0, block_count - 1) * block_cols
        initial = lax.dynamic_slice_in_dim(left_start, offset, block_cols, 2)
        incoming = jnp.where(col_index == 0, initial, received)
        extended = padded_2(incoming, (("sec", 0),), PAN)
        mix_block = lax.dynamic_slice_in_dim(mixing, offset, block_cols, 3)
        produced = advance(extended, mix_block, band_rows, sign_table)
        updated = lax.dynamic_update_slice_in_dim(sketch_out, produced, offset, 2)
        sketch_out = jnp.where(active, updated, sketch_out)
        passed = shifted(produced, "col", 1)
        return (passed, sketch_out)

    start_carry = (
        jnp.zeros((row_count, leg_count, block_cols), jnp.bfloat16),
        jnp.zeros((row_count, leg_count, rank_total), jnp.bfloat16),
    )
    passed, sketch_out = lax.fori_loop(0, step_count, turn, start_carry)
    flattened = sketch_out.reshape(row_count * leg_count, rank_total)
    row_share = rank_total // sec_count
    partial_gram = jnp.einsum("xk,xm->km", flattened, flattened, preferred_element_type=jnp.float32)
    whole_gram = lax.psum(partial_gram.astype(jnp.bfloat16), "sec").astype(jnp.float32)
    own_rows = lax.dynamic_slice_in_dim(whole_gram, lax.axis_index("sec") * row_share, row_share, 0)
    gram_out = (own_rows / (CHI * D))[None]
    return (sketch_out[None], gram_out)


def solution(mesh):
    in_specs = (
        P("sec", None, None),
        P("col", "sec", None),
        P("col", None, None, None, None),
        P("col", None, None),
        P(),
        P(),
    )
    out_specs = (P("col", "sec", None, None), P("col", "sec", None))
    return jax.shard_map(
        on_device, mesh=mesh, in_specs=in_specs, out_specs=out_specs, check_vma=False
    )
```

profile of v0, /device:TPU:0, one launch (start us, length us, event | category | flops | bytes accessed | tf_op | source)
XLA Modules:
  0.0 1914.2 jit_solution(3755021114898824152)
XLA Ops:
  20.8 1818.2 %while.17 = (s32[]{:T(128)}, bf16[512,6,128]{0,2,1:T(8,128)(2,1)S(1)}, bf16[512,6,1024]{0,2,1:T(8,128)(2,1)}, s32[]{:T(128)}, f32[6,6,6,1024]{3,2,1,0:T(8,128)},...) while((s32[]{:T(128)}, ...), condition=%wide.region_1.2_spmd.clone, body=%wide.region_0.1_spmd.clone.sunk | while | flops 2079326336 | bytes 199914256 | solution.py:95
  45.5 18.8 copy.74
  166.7 18.8 copy.74
  287.4 18.8 copy.74
  306.3 18.0 reshape.47
  408.0 18.8 copy.74
  426.9 18.0 reshape.47
  529.5 18.8 copy.74
  548.4 18.0 reshape.47
  651.0 18.8 copy.74
  669.9 18.0 reshape.47
  772.5 18.8 copy.74
  791.3 18.0 reshape.47
  893.9 18.8 copy.74
  912.8 18.0 reshape.47
  1015.3 18.8 copy.74
  1136.5 18.8 copy.74
  1155.4 18.0 reshape.47
  1257.8 18.8 copy.74
  1379.0 18.8 copy.74
  1500.2 18.8 copy.74
  1621.4 18.8 copy.74
  1742.6 18.8 copy.74
  1859.3 46.0 %all-reduce.3.cloned.1.call-done = bf16[1024,1024]{1,0:T(8,128)(2,1)} async-done(((bf16[1024,1024]{1,0:T(8,128)(2,1)}), bf16[1024,1024]{1,0:T(8,128)(2,1)}) %all-reduce.3.cloned.1.call-update) | async-done | bytes 2097168 | tf_op jit(solution)/shard_map/psum | solution.py:99
  (461 shorter events, 1443.0 us)
Async XLA Ops:
  7.2 1898.1 %all-reduce.3.cloned.1.call-start = ((), (), s32[]{:S(2)}) async-start(), calls=%async_computation | async-start | bytes 4194304 | tf_op jit(solution)/shard_map/psum | solution.py:99
  119.7 22.6 %collective-permute-start.2 = (bf16[512,6,128]{0,2,1:T(8,128)(2,1)S(1)}, bf16[512,6,128]{0,2,1:T(8,128)(2,1)S(1)}, u32[]{:S(2)}, u32[]{:S(2)}) collective-permute-start(bf16[512,6,128]{0,2,1:T(8,128)(2,1)S(1)} %reshape.48), channel_id=1, source_target_pairs={{0,4},{4,8},{8,12},{12,16},{16,20},{20,24},{24,28},{1,5},{5,9},{9,... | collective-permute-start | bytes 2359304 | tf_op jit(solution)/shard_map/while/body/eval_jaxpr/ppermute | solution.py:27
  240.9 22.0 %collective-permute-start.2 = (bf16[512,6,128]{0,2,1:T(8,128)(2,1)S(1)}, bf16[512,6,128]{0,2,1:T(8,128)(2,1)S(1)}, u32[]{:S(2)}, u32[]{:S(2)}) collective-permute-start(bf16[512,6,128]{0,2,1:T(8,128)(2,1)S(1)} %reshape.48), channel_id=1, source_target_pairs={{0,4},{4,8},{8,12},{12,16},{16,20},{20,24},{24,28},{1,5},{5,9},{9,... | collective-permute-start | bytes 2359304 | tf_op jit(solution)/shard_map/while/body/eval_jaxpr/ppermute | solution.py:27
  361.6 21.6 %collective-permute-start.2 = (bf16[512,6,128]{0,2,1:T(8,128)(2,1)S(1)}, bf16[512,6,128]{0,2,1:T(8,128)(2,1)S(1)}, u32[]{:S(2)}, u32[]{:S(2)}) collective-permute-start(bf16[512,6,128]{0,2,1:T(8,128)(2,1)S(1)} %reshape.48), channel_id=1, source_target_pairs={{0,4},{4,8},{8,12},{12,16},{16,20},{20,24},{24,28},{1,5},{5,9},{9,... | collective-permute-start | bytes 2359304 | tf_op jit(solution)/shard_map/while/body/eval_jaxpr/ppermute | solution.py:27
  482.2 22.4 %collective-permute-start.2 = (bf16[512,6,128]{0,2,1:T(8,128)(2,1)S(1)}, bf16[512,6,128]{0,2,1:T(8,128)(2,1)S(1)}, u32[]{:S(2)}, u32[]{:S(2)}) collective-permute-start(bf16[512,6,128]{0,2,1:T(8,128)(2,1)S(1)} %reshape.48), channel_id=1, source_target_pairs={{0,4},{4,8},{8,12},{12,16},{16,20},{20,24},{24,28},{1,5},{5,9},{9,... | collective-permute-start | bytes 2359304 | tf_op jit(solution)/shard_map/while/body/eval_jaxpr/ppermute | solution.py:27
  508.2 8.3 collective-permute-start
  603.7 22.4 %collective-permute-start.2 = (bf16[512,6,128]{0,2,1:T(8,128)(2,1)S(1)}, bf16[512,6,128]{0,2,1:T(8,128)(2,1)S(1)}, u32[]{:S(2)}, u32[]{:S(2)}) collective-permute-start(bf16[512,6,128]{0,2,1:T(8,128)(2,1)S(1)} %reshape.48), channel_id=1, source_target_pairs={{0,4},{4,8},{8,12},{12,16},{16,20},{20,24},{24,28},{1,5},{5,9},{9,... | collective-permute-start | bytes 2359304 | tf_op jit(solution)/shard_map/while/body/eval_jaxpr/ppermute | solution.py:27
  629.7 8.3 collective-permute-start
  725.2 22.4 %collective-permute-start.2 = (bf16[512,6,128]{0,2,1:T(8,128)(2,1)S(1)}, bf16[512,6,128]{0,2,1:T(8,128)(2,1)S(1)}, u32[]{:S(2)}, u32[]{:S(2)}) collective-permute-start(bf16[512,6,128]{0,2,1:T(8,128)(2,1)S(1)} %reshape.48), channel_id=1, source_target_pairs={{0,4},{4,8},{8,12},{12,16},{16,20},{20,24},{24,28},{1,5},{5,9},{9,... | collective-permute-start | bytes 2359304 | tf_op jit(solution)/shard_map/while/body/eval_jaxpr/ppermute | solution.py:27
  751.2 8.3 collective-permute-start
  846.7 22.3 %collective-permute-start.2 = (bf16[512,6,128]{0,2,1:T(8,128)(2,1)S(1)}, bf16[512,6,128]{0,2,1:T(8,128)(2,1)S(1)}, u32[]{:S(2)}, u32[]{:S(2)}) collective-permute-start(bf16[512,6,128]{0,2,1:T(8,128)(2,1)S(1)} %reshape.48), channel_id=1, source_target_pairs={{0,4},{4,8},{8,12},{12,16},{16,20},{20,24},{24,28},{1,5},{5,9},{9,... | collective-permute-start | bytes 2359304 | tf_op jit(solution)/shard_map/while/body/eval_jaxpr/ppermute | solution.py:27
  872.6 8.3 collective-permute-start
  968.1 22.3 %collective-permute-start.2 = (bf16[512,6,128]{0,2,1:T(8,128)(2,1)S(1)}, bf16[512,6,128]{0,2,1:T(8,128)(2,1)S(1)}, u32[]{:S(2)}, u32[]{:S(2)}) collective-permute-start(bf16[512,6,128]{0,2,1:T(8,128)(2,1)S(1)} %reshape.48), channel_id=1, source_target_pairs={{0,4},{4,8},{8,12},{12,16},{16,20},{20,24},{24,28},{1,5},{5,9},{9,... | collective-permute-start | bytes 2359304 | tf_op jit(solution)/shard_map/while/body/eval_jaxpr/ppermute | solution.py:27
  994.0 8.3 collective-permute-start
  1089.5 22.2 %collective-permute-start.2 = (bf16[512,6,128]{0,2,1:T(8,128)(2,1)S(1)}, bf16[512,6,128]{0,2,1:T(8,128)(2,1)S(1)}, u32[]{:S(2)}, u32[]{:S(2)}) collective-permute-start(bf16[512,6,128]{0,2,1:T(8,128)(2,1)S(1)} %reshape.48), channel_id=1, source_target_pairs={{0,4},{4,8},{8,12},{12,16},{16,20},{20,24},{24,28},{1,5},{5,9},{9,... | collective-permute-start | bytes 2359304 | tf_op jit(solution)/shard_map/while/body/eval_jaxpr/ppermute | solution.py:27
  1115.2 8.3 collective-permute-start
  1210.7 22.1 %collective-permute-start.2 = (bf16[512,6,128]{0,2,1:T(8,128)(2,1)S(1)}, bf16[512,6,128]{0,2,1:T(8,128)(2,1)S(1)}, u32[]{:S(2)}, u32[]{:S(2)}) collective-permute-start(bf16[512,6,128]{0,2,1:T(8,128)(2,1)S(1)} %reshape.48), channel_id=1, source_target_pairs={{0,4},{4,8},{8,12},{12,16},{16,20},{20,24},{24,28},{1,5},{5,9},{9,... | collective-permute-start | bytes 2359304 | tf_op jit(solution)/shard_map/while/body/eval_jaxpr/ppermute | solution.py:27
  1236.5 8.3 collective-permute-start
  1332.0 22.2 %collective-permute-start.2 = (bf16[512,6,128]{0,2,1:T(8,128)(2,1)S(1)}, bf16[512,6,128]{0,2,1:T(8,128)(2,1)S(1)}, u32[]{:S(2)}, u32[]{:S(2)}) collective-permute-start(bf16[512,6,128]{0,2,1:T(8,128)(2,1)S(1)} %reshape.48), channel_id=1, source_target_pairs={{0,4},{4,8},{8,12},{12,16},{16,20},{20,24},{24,28},{1,5},{5,9},{9,... | collective-permute-start | bytes 2359304 | tf_op jit(solution)/shard_map/while/body/eval_jaxpr/ppermute | solution.py:27
  1453.2 22.2 %collective-permute-start.2 = (bf16[512,6,128]{0,2,1:T(8,128)(2,1)S(1)}, bf16[512,6,128]{0,2,1:T(8,128)(2,1)S(1)}, u32[]{:S(2)}, u32[]{:S(2)}) collective-permute-start(bf16[512,6,128]{0,2,1:T(8,128)(2,1)S(1)} %reshape.48), channel_id=1, source_target_pairs={{0,4},{4,8},{8,12},{12,16},{16,20},{20,24},{24,28},{1,5},{5,9},{9,... | collective-permute-start | bytes 2359304 | tf_op jit(solution)/shard_map/while/body/eval_jaxpr/ppermute | solution.py:27
  1574.4 22.2 %collective-permute-start.2 = (bf16[512,6,128]{0,2,1:T(8,128)(2,1)S(1)}, bf16[512,6,128]{0,2,1:T(8,128)(2,1)S(1)}, u32[]{:S(2)}, u32[]{:S(2)}) collective-permute-start(bf16[512,6,128]{0,2,1:T(8,128)(2,1)S(1)} %reshape.48), channel_id=1, source_target_pairs={{0,4},{4,8},{8,12},{12,16},{16,20},{20,24},{24,28},{1,5},{5,9},{9,... | collective-permute-start | bytes 2359304 | tf_op jit(solution)/shard_map/while/body/eval_jaxpr/ppermute | solution.py:27
  1695.6 22.1 %collective-permute-start.2 = (bf16[512,6,128]{0,2,1:T(8,128)(2,1)S(1)}, bf16[512,6,128]{0,2,1:T(8,128)(2,1)S(1)}, u32[]{:S(2)}, u32[]{:S(2)}) collective-permute-start(bf16[512,6,128]{0,2,1:T(8,128)(2,1)S(1)} %reshape.48), channel_id=1, source_target_pairs={{0,4},{4,8},{8,12},{12,16},{16,20},{20,24},{24,28},{1,5},{5,9},{9,... | collective-permute-start | bytes 2359304 | tf_op jit(solution)/shard_map/while/body/eval_jaxpr/ppermute | solution.py:27
  1721.3 8.3 collective-permute-start
  1816.8 22.2 %collective-permute-start.2 = (bf16[512,6,128]{0,2,1:T(8,128)(2,1)S(1)}, bf16[512,6,128]{0,2,1:T(8,128)(2,1)S(1)}, u32[]{:S(2)}, u32[]{:S(2)}) collective-permute-start(bf16[512,6,128]{0,2,1:T(8,128)(2,1)S(1)} %reshape.48), channel_id=1, source_target_pairs={{0,4},{4,8},{8,12},{12,16},{16,20},{20,24},{24,28},{1,5},{5,9},{9,... | collective-permute-start | bytes 2359304 | tf_op jit(solution)/shard_map/while/body/eval_jaxpr/ppermute | solution.py:27
  (55 other events, 333.5 us)
Sparse Core Ops, SparseCore 0:
  1850.8 54.4 all-reduce.2
where the time goes:
time: 1930 us; the launch traced here: 1910 us
  local copies, waits for them, and re-layouts  916 us (47%)
  matrix products  357 us (18%)
  waiting for transfers between devices  270 us (14%)
  other arithmetic  200 us (10%)
  starting transfers between devices  155 us (8%)
    transpose x15, local copies, waits for them, and re-layouts, advance(): jnp.einsum('adk,duek->auek', extended.astype(jnp.float32), mix_block, pre...  283 us
    reshape x15, local copies, waits for them, and re-layouts, advance(): weighted = weighted.reshape(panel_total, PAN, leg_count, leg_count * width)  271 us
    slice x60, local copies, waits for them, and re-layouts, advance(): weighted[neighbour:neighbour + panel_count]  253 us
    ppermute x15, waiting for transfers between devices, shifted(): return lax.ppermute(block, axis, route)  224 us
    dot_general x15, matrix products, advance(): jnp.einsum('adk,duek->auek', extended.astype(jnp.float32), mix_block, pre...  196 us
    dot_general x45, matrix products, advance(): jnp.einsum('pbx,pxm->pbm', band_rows[:, :, neighbour], weighted[neighbour...  147 us
    convert_element_type x15, other arithmetic, advance(): weighted.astype(jnp.bfloat16)  144 us
    ppermute x15, starting transfers between devices, shifted(): return lax.ppermute(block, axis, route)  75.4 us
  transfers between devices with their start and end apart: 46, of which 16 were waited for; matrix products, arithmetic and copies ran while one was open for 4% of the time, Pallas kernels for 0%

commit v1 on v0

--- a/solution.py
+++ b/solution.py
@@ -6,6 +6,11 @@
 CHI = 2048
 D = 6
 PAN = 128
+
+
+def add_all(value, name):
+    parts = lax.all_gather(value, name)
+    return jnp.sum(parts, axis=0)
 
 
 def padded_2(block, sides, width):
@@ -96,7 +101,7 @@
     flattened = sketch_out.reshape(row_count * leg_count, rank_total)
     row_share = rank_total // sec_count
     partial_gram = jnp.einsum("xk,xm->km", flattened, flattened, preferred_element_type=jnp.float32)
-    whole_gram = lax.psum(partial_gram.astype(jnp.bfloat16), "sec").astype(jnp.float32)
+    whole_gram = add_all(partial_gram.astype(jnp.bfloat16), "sec").astype(jnp.float32)
     own_rows = lax.dynamic_slice_in_dim(whole_gram, lax.axis_index("sec") * row_share, row_share, 0)
     gram_out = (own_rows / (CHI * D))[None]
     return (sketch_out[None], gram_out)

time: 1930 us -> 1940 us (level)
    all_gather x0 -> x1, waiting for transfers between devices: none -> 52.8 us  [add_all(): parts = lax.all_gather(value, name)]
    psum x1 -> x0, waiting for transfers between devices: 46 us -> none  [on_device(): lax.psum(partial_gram.astype(jnp.bfloat16), 'sec').astype(jnp.float32)]
where the time goes in v1:
time: 1940 us; the launch traced here: 1930 us
  local copies, waits for them, and re-layouts  916 us (47%)
  matrix products  357 us (18%)
  waiting for transfers between devices  277 us (14%)
  other arithmetic  206 us (11%)
  starting transfers between devices  155 us (8%)
    transpose x15, local copies, waits for them, and re-layouts, advance(): jnp.einsum('adk,duek->auek', extended.astype(jnp.float32), mix_block, pre...  283 us
    reshape x15, local copies, waits for them, and re-layouts, advance(): weighted = weighted.reshape(panel_total, PAN, leg_count, leg_count * width)  271 us
    slice x60, local copies, waits for them, and re-layouts, advance(): weighted[neighbour:neighbour + panel_count]  253 us
    ppermute x15, waiting for transfers between devices, shifted(): return lax.ppermute(block, axis, route)  224 us
    dot_general x15, matrix products, advance(): jnp.einsum('adk,duek->auek', extended.astype(jnp.float32), mix_block, pre...  196 us
    dot_general x45, matrix products, advance(): jnp.einsum('pbx,pxm->pbm', band_rows[:, :, neighbour], weighted[neighbour...  147 us
    convert_element_type x15, other arithmetic, advance(): weighted.astype(jnp.bfloat16)  144 us
    ppermute x15, starting transfers between devices, shifted(): return lax.ppermute(block, axis, route)  75.4 us
  transfers between devices with their start and end apart: 46, of which 16 were waited for; matrix products, arithmetic and copies ran while one was open for 4% of the time, Pallas kernels for 0%

profile of v1, /device:TPU:0, one launch (start us, length us, event | category | flops | bytes accessed | tf_op | source)
XLA Modules:
  0.0 1926.5 jit_solution(16102613750076202155)
XLA Ops:
  20.8 1818.1 %while.17 = (s32[]{:T(128)}, bf16[512,6,128]{0,2,1:T(8,128)(2,1)S(1)}, bf16[512,6,1024]{0,2,1:T(8,128)(2,1)}, s32[]{:T(128)}, f32[6,6,6,1024]{3,2,1,0:T(8,128)},...) while((s32[]{:T(128)}, ...), condition=%wide.region_1.2_spmd.clone, body=%wide.region_0.1_spmd.clone.sunk | while | flops 2079326336 | bytes 199914256 | solution.py:100
  45.5 18.8 copy.74
  64.3 18.0 reshape.48
  166.7 18.8 copy.74
  185.6 18.0 reshape.48
  287.4 18.8 copy.74
  306.3 18.0 reshape.48
  408.0 18.8 copy.74
  426.9 18.0 reshape.48
  529.5 18.8 copy.74
  651.0 18.8 copy.74
  772.5 18.8 copy.74
  791.3 18.0 reshape.48
  893.9 18.8 copy.74
  912.7 18.0 reshape.48
  1015.2 18.8 copy.74
  1136.5 18.8 copy.74
  1257.7 18.8 copy.74
  1276.6 18.0 reshape.48
  1378.9 18.8 copy.74
  1500.1 18.8 copy.74
  1621.4 18.8 copy.74
  1742.6 18.8 copy.74
  1859.2 52.8 %all-gather.3.cloned.1.call-done = bf16[4096,1024]{1,0:T(8,128)(2,1)} async-done(((bf16[1024,1024]{1,0:T(8,128)(2,1)}), bf16[4096,1024]{1,0:T(8,128)(2,1)}) %all-gather.3.cloned.1.call-update) | async-done | bytes 8388624 | tf_op jit(solution)/shard_map/all_gather | solution.py:12
  (462 shorter events, 1448.4 us)
Async XLA Ops:
  7.2 1904.9 %all-gather.3.cloned.1.call-start = ((), (), s32[]{:S(2)}) async-start(), calls=%async_computation | async-start | bytes 10485760 | tf_op jit(solution)/shard_map/all_gather | solution.py:12
  119.7 22.6 %collective-permute-start.2 = (bf16[512,6,128]{0,2,1:T(8,128)(2,1)S(1)}, bf16[512,6,128]{0,2,1:T(8,128)(2,1)S(1)}, u32[]{:S(2)}, u32[]{:S(2)}) collective-permute-start(bf16[512,6,128]{0,2,1:T(8,128)(2,1)S(1)} %reshape.49), channel_id=1, source_target_pairs={{0,4},{4,8},{8,12},{12,16},{16,20},{20,24},{24,28},{1,5},{5,9},{9,... | collective-permute-start | bytes 2359304 | tf_op jit(solution)/shard_map/while/body/eval_jaxpr/ppermute | solution.py:32
  240.9 22.0 %collective-permute-start.2 = (bf16[512,6,128]{0,2,1:T(8,128)(2,1)S(1)}, bf16[512,6,128]{0,2,1:T(8,128)(2,1)S(1)}, u32[]{:S(2)}, u32[]{:S(2)}) collective-permute-start(bf16[512,6,128]{0,2,1:T(8,128)(2,1)S(1)} %reshape.49), channel_id=1, source_target_pairs={{0,4},{4,8},{8,12},{12,16},{16,20},{20,24},{24,28},{1,5},{5,9},{9,... | collective-permute-start | bytes 2359304 | tf_op jit(solution)/shard_map/while/body/eval_jaxpr/ppermute | solution.py:32
  361.6 21.6 %collective-permute-start.2 = (bf16[512,6,128]{0,2,1:T(8,128)(2,1)S(1)}, bf16[512,6,128]{0,2,1:T(8,128)(2,1)S(1)}, u32[]{:S(2)}, u32[]{:S(2)}) collective-permute-start(bf16[512,6,128]{0,2,1:T(8,128)(2,1)S(1)} %reshape.49), channel_id=1, source_target_pairs={{0,4},{4,8},{8,12},{12,16},{16,20},{20,24},{24,28},{1,5},{5,9},{9,... | collective-permute-start | bytes 2359304 | tf_op jit(solution)/shard_map/while/body/eval_jaxpr/ppermute | solution.py:32
  482.2 22.4 %collective-permute-start.2 = (bf16[512,6,128]{0,2,1:T(8,128)(2,1)S(1)}, bf16[512,6,128]{0,2,1:T(8,128)(2,1)S(1)}, u32[]{:S(2)}, u32[]{:S(2)}) collective-permute-start(bf16[512,6,128]{0,2,1:T(8,128)(2,1)S(1)} %reshape.49), channel_id=1, source_target_pairs={{0,4},{4,8},{8,12},{12,16},{16,20},{20,24},{24,28},{1,5},{5,9},{9,... | collective-permute-start | bytes 2359304 | tf_op jit(solution)/shard_map/while/body/eval_jaxpr/ppermute | solution.py:32
  603.7 22.4 %collective-permute-start.2 = (bf16[512,6,128]{0,2,1:T(8,128)(2,1)S(1)}, bf16[512,6,128]{0,2,1:T(8,128)(2,1)S(1)}, u32[]{:S(2)}, u32[]{:S(2)}) collective-permute-start(bf16[512,6,128]{0,2,1:T(8,128)(2,1)S(1)} %reshape.49), channel_id=1, source_target_pairs={{0,4},{4,8},{8,12},{12,16},{16,20},{20,24},{24,28},{1,5},{5,9},{9,... | collective-permute-start | bytes 2359304 | tf_op jit(solution)/shard_map/while/body/eval_jaxpr/ppermute | solution.py:32
  629.7 8.3 collective-permute-start
  725.2 22.4 %collective-permute-start.2 = (bf16[512,6,128]{0,2,1:T(8,128)(2,1)S(1)}, bf16[512,6,128]{0,2,1:T(8,128)(2,1)S(1)}, u32[]{:S(2)}, u32[]{:S(2)}) collective-permute-start(bf16[512,6,128]{0,2,1:T(8,128)(2,1)S(1)} %reshape.49), channel_id=1, source_target_pairs={{0,4},{4,8},{8,12},{12,16},{16,20},{20,24},{24,28},{1,5},{5,9},{9,... | collective-permute-start | bytes 2359304 | tf_op jit(solution)/shard_map/while/body/eval_jaxpr/ppermute | solution.py:32
  751.2 8.3 collective-permute-start
  846.7 22.3 %collective-permute-start.2 = (bf16[512,6,128]{0,2,1:T(8,128)(2,1)S(1)}, bf16[512,6,128]{0,2,1:T(8,128)(2,1)S(1)}, u32[]{:S(2)}, u32[]{:S(2)}) collective-permute-start(bf16[512,6,128]{0,2,1:T(8,128)(2,1)S(1)} %reshape.49), channel_id=1, source_target_pairs={{0,4},{4,8},{8,12},{12,16},{16,20},{20,24},{24,28},{1,5},{5,9},{9,... | collective-permute-start | bytes 2359304 | tf_op jit(solution)/shard_map/while/body/eval_jaxpr/ppermute | solution.py:32
  872.6 8.3 collective-permute-start
  968.1 22.3 %collective-permute-start.2 = (bf16[512,6,128]{0,2,1:T(8,128)(2,1)S(1)}, bf16[512,6,128]{0,2,1:T(8,128)(2,1)S(1)}, u32[]{:S(2)}, u32[]{:S(2)}) collective-permute-start(bf16[512,6,128]{0,2,1:T(8,128)(2,1)S(1)} %reshape.49), channel_id=1, source_target_pairs={{0,4},{4,8},{8,12},{12,16},{16,20},{20,24},{24,28},{1,5},{5,9},{9,... | collective-permute-start | bytes 2359304 | tf_op jit(solution)/shard_map/while/body/eval_jaxpr/ppermute | solution.py:32
  993.9 8.3 collective-permute-start
  1089.4 22.2 %collective-permute-start.2 = (bf16[512,6,128]{0,2,1:T(8,128)(2,1)S(1)}, bf16[512,6,128]{0,2,1:T(8,128)(2,1)S(1)}, u32[]{:S(2)}, u32[]{:S(2)}) collective-permute-start(bf16[512,6,128]{0,2,1:T(8,128)(2,1)S(1)} %reshape.49), channel_id=1, source_target_pairs={{0,4},{4,8},{8,12},{12,16},{16,20},{20,24},{24,28},{1,5},{5,9},{9,... | collective-permute-start | bytes 2359304 | tf_op jit(solution)/shard_map/while/body/eval_jaxpr/ppermute | solution.py:32
  1115.2 8.3 collective-permute-start
  1210.7 22.1 %collective-permute-start.2 = (bf16[512,6,128]{0,2,1:T(8,128)(2,1)S(1)}, bf16[512,6,128]{0,2,1:T(8,128)(2,1)S(1)}, u32[]{:S(2)}, u32[]{:S(2)}) collective-permute-start(bf16[512,6,128]{0,2,1:T(8,128)(2,1)S(1)} %reshape.49), channel_id=1, source_target_pairs={{0,4},{4,8},{8,12},{12,16},{16,20},{20,24},{24,28},{1,5},{5,9},{9,... | collective-permute-start | bytes 2359304 | tf_op jit(solution)/shard_map/while/body/eval_jaxpr/ppermute | solution.py:32
  1236.4 8.3 collective-permute-start
  1331.9 22.2 %collective-permute-start.2 = (bf16[512,6,128]{0,2,1:T(8,128)(2,1)S(1)}, bf16[512,6,128]{0,2,1:T(8,128)(2,1)S(1)}, u32[]{:S(2)}, u32[]{:S(2)}) collective-permute-start(bf16[512,6,128]{0,2,1:T(8,128)(2,1)S(1)} %reshape.49), channel_id=1, source_target_pairs={{0,4},{4,8},{8,12},{12,16},{16,20},{20,24},{24,28},{1,5},{5,9},{9,... | collective-permute-start | bytes 2359304 | tf_op jit(solution)/shard_map/while/body/eval_jaxpr/ppermute | solution.py:32
  1453.1 22.1 %collective-permute-start.2 = (bf16[512,6,128]{0,2,1:T(8,128)(2,1)S(1)}, bf16[512,6,128]{0,2,1:T(8,128)(2,1)S(1)}, u32[]{:S(2)}, u32[]{:S(2)}) collective-permute-start(bf16[512,6,128]{0,2,1:T(8,128)(2,1)S(1)} %reshape.49), channel_id=1, source_target_pairs={{0,4},{4,8},{8,12},{12,16},{16,20},{20,24},{24,28},{1,5},{5,9},{9,... | collective-permute-start | bytes 2359304 | tf_op jit(solution)/shard_map/while/body/eval_jaxpr/ppermute | solution.py:32
  1478.8 8.3 collective-permute-start
  1574.3 22.1 %collective-permute-start.2 = (bf16[512,6,128]{0,2,1:T(8,128)(2,1)S(1)}, bf16[512,6,128]{0,2,1:T(8,128)(2,1)S(1)}, u32[]{:S(2)}, u32[]{:S(2)}) collective-permute-start(bf16[512,6,128]{0,2,1:T(8,128)(2,1)S(1)} %reshape.49), channel_id=1, source_target_pairs={{0,4},{4,8},{8,12},{12,16},{16,20},{20,24},{24,28},{1,5},{5,9},{9,... | collective-permute-start | bytes 2359304 | tf_op jit(solution)/shard_map/while/body/eval_jaxpr/ppermute | solution.py:32
  1695.6 22.1 %collective-permute-start.2 = (bf16[512,6,128]{0,2,1:T(8,128)(2,1)S(1)}, bf16[512,6,128]{0,2,1:T(8,128)(2,1)S(1)}, u32[]{:S(2)}, u32[]{:S(2)}) collective-permute-start(bf16[512,6,128]{0,2,1:T(8,128)(2,1)S(1)} %reshape.49), channel_id=1, source_target_pairs={{0,4},{4,8},{8,12},{12,16},{16,20},{20,24},{24,28},{1,5},{5,9},{9,... | collective-permute-start | bytes 2359304 | tf_op jit(solution)/shard_map/while/body/eval_jaxpr/ppermute | solution.py:32
  1721.3 8.3 collective-permute-start
  1816.8 22.1 %collective-permute-start.2 = (bf16[512,6,128]{0,2,1:T(8,128)(2,1)S(1)}, bf16[512,6,128]{0,2,1:T(8,128)(2,1)S(1)}, u32[]{:S(2)}, u32[]{:S(2)}) collective-permute-start(bf16[512,6,128]{0,2,1:T(8,128)(2,1)S(1)} %reshape.49), channel_id=1, source_target_pairs={{0,4},{4,8},{8,12},{12,16},{16,20},{20,24},{24,28},{1,5},{5,9},{9,... | collective-permute-start | bytes 2359304 | tf_op jit(solution)/shard_map/while/body/eval_jaxpr/ppermute | solution.py:32
  (55 other events, 333.4 us)
Sparse Core Ops, SparseCore 0:
  1850.7 61.2 all-gather.2
